TPU v7x, 256 devices: a whole 4x4x8 slice. The times are simulated.
256 devices in a mesh: blk: 32 (over z, y_hi, core), rep: 8 (over x, y_lo).
Axes of the slice: x: 4, y: 4 (y_hi: 2, y_lo: 2; y = y_hi * 2 + y_lo), z: 8, core: 2. Of those that a mesh axis runs over, the one named last changes fastest.
Arguments:
- features: bfloat16 [32768, 512], P('blk'), may hold values from -6 to 6
- layer_weight: bfloat16 [512, 512], replicated, may hold values from -0.25 to 0.25
- adjacency_tiles: bfloat16 [32, 32, 8, 128, 128], P('blk', 'rep'), may hold values from -0.125 to 0.125
- tile_slots: int32 [32, 32, 8], P('blk', 'rep'), may hold values from 0 to 63, as said below
- tile_counts: int32 [32, 32], P('blk', 'rep'), may hold values from 1 to 8, as said below
- cotangent: bfloat16 [32768, 512], P('blk'), may hold values from -6 to 6
Outputs:
- activated: bfloat16 [32768, 512], P('blk')
- grad_input: bfloat16 [32768, 512], P('blk')
- grad_weight: float32 [512, 512], replicated
Inputs may be any that keep to these rules, and one draw needn't show every extreme that they name: `tile_slots`: the 8 entries of one list are distinct; entry v names row tile v // 8 and column tile v % 8. Only the first tile_counts[b, j] entries of list (b, j) are live; some list is full.
All inputs are finite; a program needn't handle non-finite values.
Results may differ from a plain program's by a relative error of at most 0.0065.
Values may be sent and summed in bfloat16 or wider, within the bound.
A program may use at most 64 MiB of HBM per device.

v0:
```python
import math

import jax
import jax.numpy as jnp
from jax import lax
from jax.experimental import pallas as pl
from jax.experimental.pallas import tpu as pltpu
from jax.sharding import PartitionSpec as P

MESH = pl.DeviceIdType.MESH
F32, BF16 = jnp.float32, jnp.bfloat16
FEATURES = 512
TILE = 128
TILES = 8
SLOTS = 8
ROWS = 1024
GROUP = 256
GROUPS = ROWS // GROUP
PARTS = 4
WIDTH = FEATURES // PARTS
K0 = math.sqrt(2.0 / math.pi)
K1 = 0.044715


def tile_rows(t):
    return pl.ds(pl.multiple_of(t * TILE, TILE), TILE)


def group_rows(g):
    return pl.ds(pl.multiple_of(g * GROUP, GROUP), GROUP)


def part_rows(p):
    return pl.ds(pl.multiple_of(p * 16, 16), 16)


def columns_of(h):
    return pl.ds(h * WIDTH, WIDTH)


def remote(src, dst, send, recv, blk, rep):
    return pltpu.make_async_remote_copy(
        src_ref=src, dst_ref=dst, send_sem=send, recv_sem=recv,
        device_id=(blk, rep), device_id_type=MESH,
    )


def landed(dst, sem):
    pltpu.make_async_copy(dst, dst, sem).wait()


def dot(a, b):
    return jnp.dot(a, b, preferred_element_type=F32)


def kernel(
    feat, w_in, tiles, slots, counts, cot_in, act_out, gin, gw,
    w, wt, cot, act, tl, tt, inv, invv, invs, dense, denset, ring, blocks, acc, part, parts, agg, back,
    sib_out, sib_in, own_out, heap, total, hop_out, hop_in, grad,
    gw_part, gw_send, gw_recv, gw_half, gw_quarter, gw_ring, gw_fin,
    in_s, out_s,
    t_s, t_r, i_s, i_r, i_l, z_s, z_r, f_s, f_r, s_s, s_r, p_s, p_r, a_s, a_r,
    b_s, b_r, o_s, o_r, h_s, h_r, g_s, g_r,
    wx_s, wx_r, wq_s, wq_r, wz_s, wz_r, wf_s, wf_r, wy_s, wy_r,
):
    b = lax.axis_index("blk")
    r = lax.axis_index("rep")
    z, q = b // 4, b % 4
    yh, core = q // 2, q % 2
    me = yh * 8 + r
    sib = b + 1 - 2 * core
    up = ((z + 1) % 8) * 4 + q
    down = ((z + 7) % 8) * 4 + q
    mine = tile_rows(r)
    low, high = pl.ds(0, TILE // 2), pl.ds(TILE // 2, TILE // 2)

    def plane(y):
        return 4 * z + 2 * y + core

    def along(d):
        return ((z + d) % 8) * 4 + q

    barrier = pltpu.get_barrier_semaphore()
    pl.semaphore_signal(barrier, inc=1, device_id=(sib, r), device_id_type=MESH)

    @pl.loop(1, 8)
    def _(d):
        pl.semaphore_signal(barrier, inc=1, device_id=(along(d), r), device_id_type=MESH)

    @pl.loop(1, 16)
    def _(i):
        p = (me + i) % 16
        pl.semaphore_signal(barrier, inc=1, device_id=(plane(p // 8), p % 8), device_id_type=MESH)

    take_w = pltpu.make_async_copy(w_in, w, in_s.at[0])
    take_w.start()
    take_cot = pltpu.make_async_copy(cot_in, cot, in_s.at[1])
    take_cot.start()
    lane = lax.broadcasted_iota(jnp.int32, (8, TILE), 1)
    for s in range(4):
        index = jnp.full((8, TILE), SLOTS, jnp.int32)
        for k in range(SLOTS):
            index = jnp.where((lane == slots[s, k]) & (k < counts[0, s]), k, index)
        inv[s] = index
    pl.semaphore_wait(barrier, 23)

    sent = []

    def later(what, sem):
        sent.append(lambda: landed(what, sem))

    def peer(i):
        return (me + i) % 16

    def fellow(i):
        return (r + jnp.where(core == 0, i, 8 - i)) % 8

    def giver(i):
        return (r + jnp.where(core == 0, 8 - i, i)) % 8

    def own(h):
        return feat.at[mine, columns_of(h)]

    def shifted(d, y):
        return jnp.where((q == 3) & (y == 0), (d + 1) % 8, d)

    def spread(h, d):
        src = own(h) if d == 0 else ring.at[h, d]
        dst = blocks.at[h, q, mine]
        if d == 0:
            y = 1 - yh
            remote(src, dst, f_s.at[h], f_r.at[h, yh], plane(y), shifted(0, y)).start()

            @pl.when(r == 0)
            def _():
                pltpu.make_async_copy(
                    feat.at[:, columns_of(h)], blocks.at[h, q], f_r.at[h, yh]
                ).start()

            return
        for y in range(2):
            to = shifted(d, y)
            here = (yh == y) & (r == to)

            @pl.when(here)
            def _():
                pltpu.make_async_copy(src, dst, f_r.at[h, yh]).start()

            @pl.when(jnp.logical_not(here))
            def _():
                remote(src, dst, f_s.at[h], f_r.at[h, yh], plane(y), to).start()

    for h in range(PARTS):
        remote(own(h), ring.at[h, 1], z_s.at[h], z_r.at[h, 1], down, r).start()
        remote(own(h), ring.at[h, 7], z_s.at[h], z_r.at[h, 7], up, r).start()
    for m in range(4):
        off = q - 2 + m
        turn = jnp.where(off < -1, -1, jnp.where(off >= 4, 1, 0))
        slot = (off + 4) % 4
        to = (r + turn + 8) % 8

        @pl.when(turn == 0)
        def _():
            pltpu.make_async_copy(tiles.at[m], tl.at[slot, pl.ds(0, SLOTS)], t_r.at[slot]).start()
            pltpu.make_async_copy(inv.at[m], invv.at[slot], i_r.at[slot]).start()

        @pl.when(turn != 0)
        def _():
            remote(tiles.at[m], tl.at[slot, pl.ds(0, SLOTS)], t_s.at[m], t_r.at[slot], b, to).start()
            remote(inv.at[m], invv.at[slot], i_s.at[m], i_r.at[slot], b, to).start()

    def forward_ring(h, k):
        landed(ring.at[h, k], z_r.at[h, k])
        landed(ring.at[h, 8 - k], z_r.at[h, 8 - k])
        if k < 3:
            remote(ring.at[h, k], ring.at[h, k + 1], z_s.at[h], z_r.at[h, k + 1], down, r).start()
            remote(ring.at[h, 8 - k], ring.at[h, 7 - k], z_s.at[h], z_r.at[h, 7 - k], up, r).start()
        else:
            remote(ring.at[h, 3, low], ring.at[h, 4, low], z_s.at[h], z_r.at[h, 4], down, r).start()
            remote(ring.at[h, 5, high], ring.at[h, 4, high], z_s.at[h], z_r.at[h, 0], up, r).start()

    def last_of_ring(h):
        landed(ring.at[h, 4, low], z_r.at[h, 4])
        landed(ring.at[h, 4, high], z_r.at[h, 0])

    for turn in range(PARTS + 4):
        for h in range(PARTS):
            k = turn - h
            if k == 0:
                spread(h, 0)
            elif 1 <= k <= 3:
                forward_ring(h, k)
                spread(h, k)
                spread(h, 8 - k)
            elif k == 4:
                last_of_ring(h)
                spread(h, 4)
    for h in range(PARTS):
        later(ring.at[h, pl.ds(0, 7)], z_s.at[h])

    def features_sent():
        for count, which in ((15, r == 0), (14, r != 0)):
            @pl.when(which)
            def _():
                for h in range(PARTS):
                    landed(heap.at[h, pl.ds(0, count)], f_s.at[h])

    sent.append(features_sent)

    def lists_sent():
        for m in range(4):
            off = q - 2 + m

            @pl.when((off < -1) | (off >= 4))
            def _():
                landed(tiles.at[m], t_s.at[m])
                landed(inv.at[m], i_s.at[m])

    sent.append(lists_sent)
    take_w.wait()
    wt[...] = w[...].T
    for s in range(4):
        landed(tl.at[s, pl.ds(0, SLOTS)], t_r.at[s])
        landed(invv.at[s], i_r.at[s])
    move = pltpu.make_async_copy(invv, invs, i_l.at[0])
    move.start()
    zero = jnp.zeros((TILE, TILE), BF16)
    for s in range(4):
        tl[s, SLOTS] = zero
        tt[s, SLOTS] = zero

    move.wait()

    @pl.loop(0, 4 * TILES)
    def _(i):
        s, t = i // TILES, i % TILES
        for c in range(TILES):
            dense[s, tile_rows(t), c * TILE:(c + 1) * TILE] = tl[s, invs[s, 0, t * TILES + c]]

    def transpose_list(s):
        @pl.loop(0, SLOTS)
        def _(i):
            tt[s, i] = tl[s, i].T

        @pl.loop(0, TILES)
        def _(t):
            for c in range(TILES):
                denset[s, tile_rows(t), c * TILE:(c + 1) * TILE] = tt[s, invs[s, 0, c * TILES + t]]

    take_cot.wait()

    def pass_on(h):
        for y in range(2):
            piece = blocks.at[h, 2 * y + core]
            landed(piece, f_r.at[h, y])
            remote(piece, piece, s_s.at[h], s_r.at[h], sib, r).start()

        later(heap.at[h], s_s.at[h])

    def own_blocks(h):
        @pl.loop(0, GROUPS)
        def _(g):
            rows = group_rows(g)
            acc[h, rows] = dot(dense[core, rows, :], blocks[h, core]) + dot(
                dense[2 + core, rows, :], blocks[h, 2 + core]
            )

    def sibling_blocks(h):
        landed(heap.at[h], s_r.at[h])

        @pl.loop(0, GROUPS)
        def _(i):
            g = (r // 2 + jnp.where(core == 0, 1 + i, 3 - i)) % GROUPS
            rows = group_rows(g)
            value = dot(dense[1 - core, rows, :], blocks[h, 1 - core]) + dot(
                dense[3 - core, rows, :], blocks[h, 3 - core]
            )
            part[h, rows] = (acc[h, rows] + value).astype(BF16)
            for j in range(2):
                t = 2 * g + j

                @pl.when(t != r)
                def _():
                    remote(part.at[h, tile_rows(t)], parts.at[h, r], p_s.at[h], p_r.at[h], b, t).start()

        later(parts.at[h, pl.ds(0, 7)], p_s.at[h])

    def add_parts(h):
        landed(parts.at[h, pl.ds(0, 7)], p_r.at[h])
        acc[h, 0:TILE] = part[h, mine].astype(F32)

        @pl.loop(1, 8)
        def _(i):
            acc[h, 0:TILE] += parts[h, giver(i)].astype(F32)

        agg[h, mine] = acc[h, 0:TILE].astype(BF16)

    def share(h):
        @pl.loop(1, 8)
        def _(i):
            t = fellow(i)
            remote(agg.at[h, mine], agg.at[h, mine], a_s.at[h], a_r.at[r], b, t).start()

        later(parts.at[h, pl.ds(0, 7)], a_s.at[h])

    for h in range(PARTS):
        if h > 0:
            transpose_list(h - 1)
        pass_on(h)
        own_blocks(h)
        sibling_blocks(h)
        if h >= 2:
            add_parts(h - 2)
            share(h - 2)
    for h in range(PARTS - 2, PARTS):
        add_parts(h)
        share(h)
    transpose_list(3)

    def chunk(c):
        rows = tile_rows(c)
        inputs = jnp.concatenate([agg[h, rows] for h in range(PARTS)], axis=1)
        pre = dot(inputs, w[...])
        square = pre * pre
        t = jnp.tanh(K0 * (pre + K1 * square * pre))
        half = 0.5 * (1.0 + t)
        act[rows] = (pre * half).astype(BF16)
        pltpu.make_async_copy(act.at[rows], act_out.at[rows], out_s.at[0]).start()
        slope = half + 0.5 * pre * (1.0 - t * t) * (K0 * (1.0 + 3.0 * K1 * square))
        delta = (cot[rows].astype(F32) * slope).astype(BF16)
        value = dot(delta, wt[...]).astype(BF16)
        for h in range(PARTS):
            back[h, rows] = value[:, h * WIDTH:(h + 1) * WIDTH]
        return inputs, delta

    gw_part[...] = lax.dot_general(
        *chunk(r), (((0,), (0,)), ((), ())), preferred_element_type=F32
    )
    gw_send[...] = gw_part[group_rows(1 - core)].astype(BF16)
    remote(gw_send, gw_recv, wx_s.at[0], wx_r.at[0], sib, r).start()
    later(gw_send, wx_s.at[0])

    @pl.loop(1, 8)
    def _(i):
        c = giver(i)
        landed(agg.at[0, pl.ds(0, PARTS * TILE)], a_r.at[c])
        chunk(c)

    landed(gw_recv, wx_r.at[0])
    gw_half[...] = (gw_part[group_rows(core)] + gw_recv[...].astype(F32)).astype(BF16)

    @pl.loop(1, 16)
    def _(i):
        p = (me + i) % 16
        remote(
            gw_half.at[part_rows(p)], gw_quarter.at[part_rows(me)], wq_s.at[0], wq_r.at[0],
            plane(p // 8), p % 8,
        ).start()

    later(gw_half.at[pl.ds(0, 240)], wq_s.at[0])
    def side_by_side(ref, pair, *at):
        return jnp.concatenate([ref[(2 * pair, *at)], ref[(2 * pair + 1, *at)]], axis=1)

    def sibling_grads(pair):
        @pl.loop(0, 2 * GROUPS)
        def _(i):
            y, g = i // GROUPS, i % GROUPS
            rows = group_rows(g)
            value = dot(denset[2 * y + 1 - core, rows, :], side_by_side(back, pair)).astype(BF16)
            for n in range(2):
                h = 2 * pair + n
                sib_out[h, y, rows] = value[:, n * WIDTH:(n + 1) * WIDTH]
                remote(
                    sib_out.at[h, y, rows], sib_in.at[h, y, rows], b_s.at[h], b_r.at[h], sib, r
                ).start()

        for n in range(2):
            later(sib_out.at[2 * pair + n], b_s.at[2 * pair + n])

    def own_grads(pair):
        for n in range(2):
            landed(sib_in.at[2 * pair + n], b_r.at[2 * pair + n])

        @pl.loop(0, 2 * GROUPS)
        def _(i):
            j = i % 4
            y, g = (i + i // 4) % 2, (r // 2 + 2 * j + 1 + 5 * (j // 2)) % GROUPS
            rows = group_rows(g)
            value = dot(denset[2 * y + core, rows, :], side_by_side(back, pair))
            turned = jnp.where((yh == 0) & (core == 1) & (y == 1), (r + 7) % 8, r)
            for n in range(2):
                h = 2 * pair + n
                own_out[h, y, rows] = (
                    value[:, n * WIDTH:(n + 1) * WIDTH] + sib_in[h, y, rows].astype(F32)
                ).astype(BF16)
                for j in range(2):
                    t = 2 * g + j
                    src, dst = own_out.at[h, y, tile_rows(t)], heap.at[h, me]
                    here = (yh == y) & (r == t)

                    @pl.when(here)
                    def _():
                        pltpu.make_async_copy(src, dst, o_r.at[h, turned]).start()

                    @pl.when(jnp.logical_not(here))
                    def _():
                        remote(src, dst, o_s.at[h], o_r.at[h, turned], plane(y), t).start()

        for n in range(2):
            later(heap.at[0, pl.ds(0, 15)], o_s.at[2 * pair + n])

    sibling_grads(0)
    sibling_grads(1)
    own_grads(0)
    own_grads(1)
    landed(gw_quarter.at[pl.ds(0, 240)], wq_r.at[0])
    gw_ring[0] = gw_half[part_rows(me)].astype(F32)

    @pl.loop(1, 16)
    def _(i):
        p = (me + i) % 16
        gw_ring[0] += gw_quarter[part_rows(p)].astype(F32)

    @pl.loop(1, 8)
    def _(d):
        remote(gw_ring.at[0], gw_ring.at[d], wz_s.at[0], wz_r.at[0], along(d), r).start()

    later(gw_ring.at[pl.ds(0, 7)], wz_s.at[0])

    def send_along(h):
        @pl.loop(0, 8)
        def _(i):
            d = 2 * ((r // 2 + 7 - i // 2 - 2 * yh) % 4) + i % 2
            first = shifted(d, 0)
            landed(heap.at[h, pl.ds(0, 2)], o_r.at[h, d])
            value = heap[h, first].astype(F32) + heap[h, 8 + d].astype(F32)

            @pl.when(d == 0)
            def _():
                total[h] = value

            @pl.when(d != 0)
            def _():
                hop_out[h, d] = value.astype(BF16)
                remote(hop_out.at[h, d], hop_in.at[h, d], h_s.at[h], h_r.at[h], along(d), r).start()

        later(ring.at[h, pl.ds(0, 7)], h_s.at[h])

    def finish(h):
        landed(hop_in.at[h, pl.ds(0, 7)], h_r.at[h])

        @pl.loop(1, 8)
        def _(d):
            total[h] += hop_in[h, d].astype(F32)

        place = grad.at[h, mine]
        grad[h, mine] = total[h].astype(BF16)

        @pl.loop(1, 8)
        def _(i):
            t = fellow(i)
            remote(place, place, g_s.at[h], g_r.at[h], b, t).start()

        later(parts.at[h, pl.ds(0, 7)], g_s.at[h])

    send_along(0)
    send_along(1)
    landed(gw_ring.at[pl.ds(0, 7)], wz_r.at[0])

    whole = gw_ring[z]
    for k in range(1, 8):
        whole = whole + gw_ring[(z + 8 - k) % 8]
    place = pl.ds(pl.multiple_of(core * 256 + me * 16, 16), 16)
    gw_fin[place] = (whole * (1.0 / math.sqrt(32 * ROWS))).astype(BF16)

    @pl.loop(1, 16)
    def _(i):
        p = (me + i) % 16
        remote(
            gw_fin.at[place], gw_fin.at[place], wf_s.at[0], wf_r.at[0], plane(p // 8), p % 8
        ).start()

    later(gw_half.at[pl.ds(0, 240)], wf_s.at[0])

    for h in range(PARTS):
        finish(h)
        if h + 2 < PARTS:
            send_along(h + 2)

    landed(gw_fin.at[pl.ds(0, 240)], wf_r.at[0])
    landed(act, out_s.at[0])

    half = group_rows(core)
    remote(gw_fin.at[half], gw_fin.at[half], wy_s.at[0], wy_r.at[0], sib, r).start()
    later(gw_fin.at[half], wy_s.at[0])
    landed(gw_fin.at[group_rows(1 - core)], wy_r.at[0])
    give_gw = pltpu.make_async_copy(gw_fin, gw, in_s.at[0])
    give_gw.start()

    for h in range(PARTS):
        landed(parts.at[h, pl.ds(0, 7)], g_r.at[h])
        pltpu.make_async_copy(grad.at[h], gin.at[:, columns_of(h)], out_s.at[h]).start()

    for wait in sent:
        wait()
    give_gw.wait()
    for h in range(PARTS):
        landed(grad.at[h], out_s.at[h])


def hand_over_kernel(act, grad, weight, act_out, grad_out, weight_out, held, narrow, wide, get, give):
    rows = ROWS // 4
    gets, gives = [], []
    for n, (src, dst) in enumerate(((act, act_out), (grad, grad_out))):
        for m in range(4):
            part, place = pl.ds(m * rows, rows), held.at[4 * n + m]
            gets.append(pltpu.make_async_copy(src.at[part], place, get.at[4 * n + m]))
            gives.append(pltpu.make_async_copy(place, dst.at[part], give.at[4 * n + m]))
    take = pltpu.make_async_copy(weight, narrow, get.at[8])
    take.start()
    for copy in gets:
        copy.start()
    take.wait()
    wide[...] = narrow[...].astype(F32)
    put = pltpu.make_async_copy(wide, weight_out, give.at[8])
    put.start()
    for first, second in zip(gets, gives):
        first.wait()
        second.start()
    for copy in gives:
        copy.wait()
    put.wait()


def hand_over(act, grad, weight):
    hbm = pl.BlockSpec(memory_space=pl.ANY)
    return pl.pallas_call(
        hand_over_kernel,
        out_shape=(
            jax.ShapeDtypeStruct((ROWS, FEATURES), BF16),
            jax.ShapeDtypeStruct((ROWS, FEATURES), BF16),
            jax.ShapeDtypeStruct((FEATURES, FEATURES), F32),
        ),
        in_specs=[hbm, hbm, hbm],
        out_specs=(hbm, hbm, hbm),
        scratch_shapes=[
            pltpu.VMEM((8, ROWS // 4, FEATURES), BF16),
            pltpu.VMEM((FEATURES, FEATURES), BF16),
            pltpu.VMEM((FEATURES, FEATURES), F32),
            pltpu.SemaphoreType.DMA((9,)),
            pltpu.SemaphoreType.DMA((9,)),
        ],
        compiler_params=pltpu.CompilerParams(vmem_limit_bytes=60 * 1024 * 1024),
        cost_estimate=pl.CostEstimate(flops=0, bytes_accessed=6 << 20, transcendentals=0),
    )(act, grad, weight)


def per_device(features, layer_weight, adjacency_tiles, tile_slots, tile_counts, cotangent):
    hbm = pl.BlockSpec(memory_space=pl.ANY)
    smem = pl.BlockSpec(memory_space=pltpu.SMEM)
    dma = pltpu.SemaphoreType.DMA
    half = (PARTS, ROWS, WIDTH)
    slices = (PARTS, 8, TILE, WIDTH)
    scratch = [
        pltpu.VMEM((FEATURES, FEATURES), BF16),
        pltpu.VMEM((FEATURES, FEATURES), BF16),
        pltpu.VMEM((ROWS, FEATURES), BF16),
        pltpu.VMEM((ROWS, FEATURES), BF16),
        pltpu.VMEM((4, SLOTS + 1, TILE, TILE), BF16),
        pltpu.VMEM((4, SLOTS + 1, TILE, TILE), BF16),
        pltpu.VMEM((4, 8, TILE), jnp.int32),
        pltpu.VMEM((4, 8, TILE), jnp.int32),
        pltpu.SMEM((4, 8, TILE), jnp.int32),
        pltpu.VMEM((4, ROWS, ROWS), BF16),
        pltpu.VMEM((4, ROWS, ROWS), BF16),
        pltpu.VMEM(slices, BF16),
        pltpu.VMEM((PARTS, 4, ROWS, WIDTH), BF16),
        pltpu.VMEM(half, F32),
        pltpu.VMEM(half, BF16),
        pltpu.VMEM(slices, BF16),
        pltpu.VMEM(half, BF16),
        pltpu.VMEM(half, BF16),
        pltpu.VMEM((PARTS, 2, ROWS, WIDTH), BF16),
        pltpu.VMEM((PARTS, 2, ROWS, WIDTH), BF16),
        pltpu.VMEM((PARTS, 2, ROWS, WIDTH), BF16),
        pltpu.VMEM((PARTS, 16, TILE, WIDTH), BF16),
        pltpu.VMEM((PARTS, TILE, WIDTH), F32),
        pltpu.VMEM(slices, BF16),
        pltpu.VMEM(slices, BF16),
        pltpu.VMEM(half, BF16),
        pltpu.VMEM((FEATURES, FEATURES), F32),
        pltpu.VMEM((256, FEATURES), BF16),
        pltpu.VMEM((256, FEATURES), BF16),
        pltpu.VMEM((256, FEATURES), BF16),
        pltpu.VMEM((256, FEATURES), BF16),
        pltpu.VMEM((8, 16, FEATURES), F32),
        pltpu.VMEM((FEATURES, FEATURES), BF16),
    ]
    two = PARTS
    two = (PARTS,)
    sems = [
        (2,), (PARTS,),
        (4,), (4,), (4,), (4,), (1,),
        two, (PARTS, 8), two, (PARTS, 2), two, two,
        two, two, two, (8,),
        two, two, two, (PARTS, 8), two, two, two, two,
        (1,), (1,), (1,), (1,), (1,), (1,), (1,), (1,), (1,), (1,),
    ]
    activated, grad_input, grad_weight = pl.pallas_call(
        kernel,
        out_shape=(
            jax.ShapeDtypeStruct((ROWS, FEATURES), BF16),
            jax.ShapeDtypeStruct((ROWS, FEATURES), BF16),
            jax.ShapeDtypeStruct((FEATURES, FEATURES), BF16),
        ),
        in_specs=[hbm, hbm, hbm, smem, smem, hbm],
        out_specs=(hbm, hbm, hbm),
        scratch_shapes=scratch + [dma(n) for n in sems],
        compiler_params=pltpu.CompilerParams(
            collective_id=0, has_side_effects=True, vmem_limit_bytes=58 * 1024 * 1024
        ),
        cost_estimate=pl.CostEstimate(
            flops=10 * 2 * ROWS * ROWS * FEATURES, bytes_accessed=8 << 20, transcendentals=ROWS * FEATURES
        ),
    )(features, layer_weight, adjacency_tiles[0], tile_slots[0], tile_counts, cotangent)
    return hand_over(activated, grad_input, grad_weight)


def solution(mesh):
    return jax.shard_map(
        per_device,
        mesh=mesh,
        in_specs=(
            P("blk", None),
            P(),
            P("blk", "rep", None, None, None),
            P("blk", "rep", None),
            P("blk", "rep"),
            P("blk", None),
        ),
        out_specs=(P("blk", None), P("blk", None), P()),
        check_vma=False,
    )
```

profile of v0, /device:TPU:19, one launch (start us, length us, event | category | flops | bytes accessed | tf_op | source)
XLA Modules:
  0.0 128.2 jit_solution(3856222184694024478)
XLA Ops:
  0.6 124.6 %shard_map.85 = (bf16[1024,512]{1,0:T(8,128)(2,1)}, bf16[1024,512]{1,0:T(8,128)(2,1)}, bf16[512,512]{1,0:T(8,128)(2,1)}) custom-call(bf16[1024,512]{1,0:T(8,128)(2,1)} %feat.1, bf16[512,512]{1,0:T(8,128)(2,1)} %w_in.1, bf16[4,8,128,128]{3,2,1,0:T(8,128)(2,1)} %bitcast.2, s32[4,8]{1,0:T(4,128)} %bitcast.3, s32[1,4]{1,0:T(1,128)} %counts.1, ...), custom_call_target="tpu_custom_call" | custom-call | flops 10737418240 | bytes 8388608 | tf_op jit(solution)/shard_map/pallas_call | solution.py:609
  125.3 2.9 %shard_map.86 = (bf16[1024,512]{1,0:T(8,128)(2,1)}, bf16[1024,512]{1,0:T(8,128)(2,1)}, f32[512,512]{1,0:T(8,128)}) custom-call(bf16[1024,512]{1,0:T(8,128)(2,1)} %get-tuple-element.6.act, bf16[1024,512]{1,0:T(8,128)(2,1)} %get-tuple-element.7.grad, bf16[512,512]{1,0:T(8,128)(2,1)} %get-tuple-element.8.weight), custom_call_target="tpu_custom_call" | custom-call | bytes 6291456 | tf_op jit(solution)/shard_map/pallas_call | solution.py:537
where the time goes:
time: 128 us
  Pallas kernels  128 us (100%)
    pallas_call x1, Pallas kernels, per_device(): pl.pallas_call(kernel, out_shape=(jax.ShapeDtypeStruct((ROWS, FEATURES),...  125 us
    pallas_call x1, Pallas kernels, hand_over(): pl.pallas_call(hand_over_kernel, out_shape=(jax.ShapeDtypeStruct((ROWS, F...  2.92 us

commit v1 on v0

--- a/solution.py
+++ b/solution.py
@@ -231,11 +231,14 @@
 
     move.wait()
 
-    @pl.loop(0, 4 * TILES)
-    def _(i):
-        s, t = i // TILES, i % TILES
-        for c in range(TILES):
-            dense[s, tile_rows(t), c * TILE:(c + 1) * TILE] = tl[s, invs[s, 0, t * TILES + c]]
+    def build(first):
+        @pl.loop(0, 2 * TILES)
+        def _(i):
+            s, t = first + 2 * (i // TILES), i % TILES
+            for c in range(TILES):
+                dense[s, tile_rows(t), c * TILE:(c + 1) * TILE] = tl[s, invs[s, 0, t * TILES + c]]
+
+    build(core)
 
     def transpose_list(s):
         @pl.loop(0, SLOTS)
@@ -308,6 +311,8 @@
             transpose_list(h - 1)
         pass_on(h)
         own_blocks(h)
+        if h == 0:
+            build(1 - core)
         sibling_blocks(h)
         if h >= 2:
             add_parts(h - 2)

time: 128 us -> 128 us (level)
  no operation moved by 1% of the time
where the time goes in v1:
time: 128 us
  Pallas kernels  128 us (100%)
    pallas_call x1, Pallas kernels, per_device(): pl.pallas_call(kernel, out_shape=(jax.ShapeDtypeStruct((ROWS, FEATURES),...  125 us
    pallas_call x1, Pallas kernels, hand_over(): pl.pallas_call(hand_over_kernel, out_shape=(jax.ShapeDtypeStruct((ROWS, F...  2.92 us

profile of v1, /device:TPU:19, one launch (start us, length us, event | category | flops | bytes accessed | tf_op | source)
XLA Modules:
  0.0 128.2 jit_solution(1381533698849693662)
XLA Ops:
  0.6 124.7 %shard_map.85 = (bf16[1024,512]{1,0:T(8,128)(2,1)}, bf16[1024,512]{1,0:T(8,128)(2,1)}, bf16[512,512]{1,0:T(8,128)(2,1)}) custom-call(bf16[1024,512]{1,0:T(8,128)(2,1)} %feat.1, bf16[512,512]{1,0:T(8,128)(2,1)} %w_in.1, bf16[4,8,128,128]{3,2,1,0:T(8,128)(2,1)} %bitcast.2, s32[4,8]{1,0:T(4,128)} %bitcast.3, s32[1,4]{1,0:T(1,128)} %counts.1, ...), custom_call_target="tpu_custom_call" | custom-call | flops 10737418240 | bytes 8388608 | tf_op jit(solution)/shard_map/pallas_call | solution.py:614
  125.3 2.9 %shard_map.86 = (bf16[1024,512]{1,0:T(8,128)(2,1)}, bf16[1024,512]{1,0:T(8,128)(2,1)}, f32[512,512]{1,0:T(8,128)}) custom-call(bf16[1024,512]{1,0:T(8,128)(2,1)} %get-tuple-element.6.act, bf16[1024,512]{1,0:T(8,128)(2,1)} %get-tuple-element.7.grad, bf16[512,512]{1,0:T(8,128)(2,1)} %get-tuple-element.8.weight), custom_call_target="tpu_custom_call" | custom-call | bytes 6291456 | tf_op jit(solution)/shard_map/pallas_call | solution.py:542
